TPU v7x, 256 devices: a whole 4x4x8 slice. The times are simulated.
256 devices in a mesh: node: 16 (over x, y), feat: 16 (over z, core).
Axes of the slice: x: 4, y: 4, z: 8, core: 2. Of those that a mesh axis runs over, the one named last changes fastest.
Arguments:
- feats_t: float32 [512, 16384], P('feat', 'node'), may hold values from -6 to 6
- weight: float32 [512, 512], P(None, 'feat'), may hold values from -0.25 to 0.25
- cot_t: float32 [512, 16384], P('feat', 'node'), may hold values from -6 to 6
- tiles: float32 [128, 8, 128, 128], P('node'), may hold values from -0.1875 to 0.1875
- col_ids: int32 [128, 8], P('node'), may hold values from 0 to 127, as said below
- counts: int32 [128], P('node'), may hold values from 1 to 8, as said below
Outputs:
- out_t: float32 [512, 16384], P('feat', 'node')
- grad_feats: float32 [512, 16384], P('feat', 'node')
- grad_weight: float32 [512, 512], P(None, 'feat')
Inputs may be any that keep to these rules, and one draw needn't show every extreme that they name: `col_ids`: column block c belongs to node index c // 8. Among the 64 slots of one node index's row blocks, at most 4 name column blocks of any one node index, and some node index is named by exactly 4; ids may repeat within a row block. `counts`: row block 0 has all 8 slots live; loads differ between devices.
All inputs are finite; a program needn't handle non-finite values.
Results may differ from a plain program's by a relative error of at most 0.0001.
Values sent between devices are 32-bit elements; how exact they have to be, the bound alone decides.
A program may use at most 64 MiB of HBM per device.

v0:
```python
import jax
import jax.numpy as jnp
from jax import lax
from jax.sharding import PartitionSpec as P

HIGH = lax.Precision.HIGHEST


def from_root(value, axis, source):
    kept = jnp.where(lax.axis_index(axis) == source, value, 0).astype(value.dtype)
    return lax.psum(kept, axis)


def on_device(feats_t, weight, cot_t, tiles, col_ids, counts):
    width_part, rows = feats_t.shape
    nblocks = tiles.shape[0]
    slots = tiles.shape[1]
    local_blocks = rows // 128
    node_count = lax.axis_size("node")
    total = local_blocks * node_count
    live = (jnp.arange(slots)[None, :] < counts[:, None]).astype(jnp.float32)
    empty = jnp.zeros((width_part, nblocks, slots, 128), jnp.float32)
    owner = col_ids // local_blocks
    within = col_ids % local_blocks

    def section(root, selected):
        received = from_root(feats_t, "node", root)
        shaped = received.reshape(width_part, local_blocks, 128)
        picked = jnp.take(shaped, within, axis=1)
        return jnp.where((owner == root)[None, :, :, None], picked, selected)

    selected = lax.fori_loop(0, node_count, section, empty)
    selected = selected * live[None, :, :, None]
    mixed_t = jnp.einsum("fbkc,bkrc->fbr", selected, tiles, precision=HIGH).reshape(
        width_part, rows
    )
    mixed_full = lax.all_gather(mixed_t, "feat", axis=0, tiled=True)
    pre_t = jnp.dot(weight.T, mixed_full, precision=HIGH)
    sig = jax.nn.sigmoid(pre_t)
    out_t = pre_t * sig
    grad_pre = cot_t * (sig * (1.0 + pre_t * (1.0 - sig)))
    grad_weight = lax.psum(jnp.dot(mixed_full, grad_pre.T, precision=HIGH), "node")
    grad_mixed = lax.psum_scatter(
        jnp.dot(weight, grad_pre, precision=HIGH), "feat", scatter_dimension=0, tiled=True
    )
    contrib = jnp.einsum(
        "fbr,bkrc->fbkc", grad_mixed.reshape(width_part, nblocks, 128), tiles, precision=HIGH
    )
    contrib = contrib * live[None, :, :, None]
    onehot = (col_ids[:, :, None] == jnp.arange(total)[None, None, :]).astype(jnp.float32)
    partial_grad = jnp.einsum("fbkc,bkj->fjc", contrib, onehot, precision=HIGH).reshape(
        width_part, total * 128
    )
    grad_feats = lax.psum_scatter(partial_grad, "node", scatter_dimension=1, tiled=True)
    return (out_t, grad_feats, grad_weight)


def solution(mesh):
    return jax.shard_map(
        on_device,
        mesh=mesh,
        in_specs=(
            P("feat", "node"),
            P(None, "feat"),
            P("feat", "node"),
            P("node", None, None, None),
            P("node", None),
            P("node"),
        ),
        out_specs=(P("feat", "node"), P("feat", "node"), P(None, "feat")),
        check_vma=False,
    )
```

profile of v0, /device:TPU:2, one launch (start us, length us, event | category | flops | bytes accessed | tf_op | source)
XLA Modules:
  0.0 1878.7 jit_solution(987238460676156024)
XLA Ops:
  9.5 1572.9 %while.16 = (s32[]{:T(128)}, f32[32,8,8,128]{3,0,2,1:T(8,128)S(1)}, s32[8,8]{1,0:T(8,128)S(1)}, s32[8,8]{1,0:T(8,128)S(1)}, f32[32,1024]{1,0:T(8,128)}, /*index=5*/s32[]{:T(128)}, u32[]{:T(128)}, u32[]{:T(128)}, s32[]{:T(128)}) while((s32[]{:T(128)}, f32[32,8,8,128]{3,0,2,1:T(8,128)S(1)}, s32[8,8]{1,0:T(8,128)S(1)}, ...), condition=%wide.region_2.3_spmd.clone, body=%wide.region_0.2_spmd.clone.sunk | while | flops 853639 | bytes 6298053 | solution.py:32
  10.4 98.7 %all-reduce.5.cloned.1.call-done = f32[32,8,128]{2,0,1:T(8,128)} async-done(((f32[32,8,128]{2,0,1:T(8,128)}), f32[32,8,128]{2,0,1:T(8,128)}) %all-reduce.5.cloned.1.call-update) | async-done | bytes 131088 | tf_op jit(solution)/shard_map/while/body/eval_jaxpr/psum | solution.py:11
  109.1 1.5 gather_fusion
  111.8 95.5 %all-reduce.5.cloned.1.call-done = f32[32,8,128]{2,0,1:T(8,128)} async-done(((f32[32,8,128]{2,0,1:T(8,128)}), f32[32,8,128]{2,0,1:T(8,128)}) %all-reduce.5.cloned.1.call-update) | async-done | bytes 131088 | tf_op jit(solution)/shard_map/while/body/eval_jaxpr/psum | solution.py:11
  207.4 1.5 gather_fusion
  210.1 95.5 %all-reduce.5.cloned.1.call-done = f32[32,8,128]{2,0,1:T(8,128)} async-done(((f32[32,8,128]{2,0,1:T(8,128)}), f32[32,8,128]{2,0,1:T(8,128)}) %all-reduce.5.cloned.1.call-update) | async-done | bytes 131088 | tf_op jit(solution)/shard_map/while/body/eval_jaxpr/psum | solution.py:11
  305.6 1.5 gather_fusion
  308.3 95.2 %all-reduce.5.cloned.1.call-done = f32[32,8,128]{2,0,1:T(8,128)} async-done(((f32[32,8,128]{2,0,1:T(8,128)}), f32[32,8,128]{2,0,1:T(8,128)}) %all-reduce.5.cloned.1.call-update) | async-done | bytes 131088 | tf_op jit(solution)/shard_map/while/body/eval_jaxpr/psum | solution.py:11
  403.6 1.5 gather_fusion
  405.5 1.6 copy_bitcast_fusion.4
  407.2 94.3 %all-reduce.5.cloned.1.call-done = f32[32,8,128]{2,0,1:T(8,128)} async-done(((f32[32,8,128]{2,0,1:T(8,128)}), f32[32,8,128]{2,0,1:T(8,128)}) %all-reduce.5.cloned.1.call-update) | async-done | bytes 131088 | tf_op jit(solution)/shard_map/while/body/eval_jaxpr/psum | solution.py:11
  501.5 1.5 gather_fusion
  504.2 95.2 %all-reduce.5.cloned.1.call-done = f32[32,8,128]{2,0,1:T(8,128)} async-done(((f32[32,8,128]{2,0,1:T(8,128)}), f32[32,8,128]{2,0,1:T(8,128)}) %all-reduce.5.cloned.1.call-update) | async-done | bytes 131088 | tf_op jit(solution)/shard_map/while/body/eval_jaxpr/psum | solution.py:11
  599.5 1.5 gather_fusion
  602.2 95.5 %all-reduce.5.cloned.1.call-done = f32[32,8,128]{2,0,1:T(8,128)} async-done(((f32[32,8,128]{2,0,1:T(8,128)}), f32[32,8,128]{2,0,1:T(8,128)}) %all-reduce.5.cloned.1.call-update) | async-done | bytes 131088 | tf_op jit(solution)/shard_map/while/body/eval_jaxpr/psum | solution.py:11
  697.7 1.5 gather_fusion
  700.5 95.5 %all-reduce.5.cloned.1.call-done = f32[32,8,128]{2,0,1:T(8,128)} async-done(((f32[32,8,128]{2,0,1:T(8,128)}), f32[32,8,128]{2,0,1:T(8,128)}) %all-reduce.5.cloned.1.call-update) | async-done | bytes 131088 | tf_op jit(solution)/shard_map/while/body/eval_jaxpr/psum | solution.py:11
  796.0 1.5 gather_fusion
  798.7 95.5 %all-reduce.5.cloned.1.call-done = f32[32,8,128]{2,0,1:T(8,128)} async-done(((f32[32,8,128]{2,0,1:T(8,128)}), f32[32,8,128]{2,0,1:T(8,128)}) %all-reduce.5.cloned.1.call-update) | async-done | bytes 131088 | tf_op jit(solution)/shard_map/while/body/eval_jaxpr/psum | solution.py:11
  894.2 1.5 gather_fusion
  897.0 95.2 %all-reduce.5.cloned.1.call-done = f32[32,8,128]{2,0,1:T(8,128)} async-done(((f32[32,8,128]{2,0,1:T(8,128)}), f32[32,8,128]{2,0,1:T(8,128)}) %all-reduce.5.cloned.1.call-update) | async-done | bytes 131088 | tf_op jit(solution)/shard_map/while/body/eval_jaxpr/psum | solution.py:11
  992.2 1.5 gather_fusion
  994.9 95.5 %all-reduce.5.cloned.1.call-done = f32[32,8,128]{2,0,1:T(8,128)} async-done(((f32[32,8,128]{2,0,1:T(8,128)}), f32[32,8,128]{2,0,1:T(8,128)}) %all-reduce.5.cloned.1.call-update) | async-done | bytes 131088 | tf_op jit(solution)/shard_map/while/body/eval_jaxpr/psum | solution.py:11
  1090.4 1.5 gather_fusion
  1093.2 95.2 %all-reduce.5.cloned.1.call-done = f32[32,8,128]{2,0,1:T(8,128)} async-done(((f32[32,8,128]{2,0,1:T(8,128)}), f32[32,8,128]{2,0,1:T(8,128)}) %all-reduce.5.cloned.1.call-update) | async-done | bytes 131088 | tf_op jit(solution)/shard_map/while/body/eval_jaxpr/psum | solution.py:11
  1188.4 1.5 gather_fusion
  1191.1 95.5 %all-reduce.5.cloned.1.call-done = f32[32,8,128]{2,0,1:T(8,128)} async-done(((f32[32,8,128]{2,0,1:T(8,128)}), f32[32,8,128]{2,0,1:T(8,128)}) %all-reduce.5.cloned.1.call-update) | async-done | bytes 131088 | tf_op jit(solution)/shard_map/while/body/eval_jaxpr/psum | solution.py:11
  1286.7 1.5 gather_fusion
  1289.4 95.2 %all-reduce.5.cloned.1.call-done = f32[32,8,128]{2,0,1:T(8,128)} async-done(((f32[32,8,128]{2,0,1:T(8,128)}), f32[32,8,128]{2,0,1:T(8,128)}) %all-reduce.5.cloned.1.call-update) | async-done | bytes 131088 | tf_op jit(solution)/shard_map/while/body/eval_jaxpr/psum | solution.py:11
  1384.6 1.5 gather_fusion
  1387.3 95.2 %all-reduce.5.cloned.1.call-done = f32[32,8,128]{2,0,1:T(8,128)} async-done(((f32[32,8,128]{2,0,1:T(8,128)}), f32[32,8,128]{2,0,1:T(8,128)}) %all-reduce.5.cloned.1.call-update) | async-done | bytes 131088 | tf_op jit(solution)/shard_map/while/body/eval_jaxpr/psum | solution.py:11
  1482.6 1.5 gather_fusion
  1485.3 95.2 %all-reduce.5.cloned.1.call-done = f32[32,8,128]{2,0,1:T(8,128)} async-done(((f32[32,8,128]{2,0,1:T(8,128)}), f32[32,8,128]{2,0,1:T(8,128)}) %all-reduce.5.cloned.1.call-update) | async-done | bytes 131088 | tf_op jit(solution)/shard_map/while/body/eval_jaxpr/psum | solution.py:11
  1580.5 1.5 gather_fusion
  1582.4 6.1 convolution_bitcast_fusion.1
  1589.3 39.5 %all-gather.2.cloned.1.call-done = f32[512,1024]{1,0:T(8,128)} async-done(((f32[32,1024]{1,0:T(8,128)}), f32[512,1024]{1,0:T(8,128)}) %all-gather.2.cloned.1.call-update) | async-done | bytes 2097168 | tf_op jit(solution)/shard_map/all_gather | solution.py:37
  1628.8 3.6 fusion.5
  1632.4 1.9 convolution_bitcast_fusion
  1634.3 1.8 copy.24
  1636.2 1.5 copy-done.1
  1637.7 2.7 fusion.12
  1640.5 53.4 %reduce-scatter.7.cloned.1.call-done = f32[32,1024]{1,0:T(8,128)} async-done(((f32[512,1024]{1,0:T(8,128)}), f32[32,1024]{1,0:T(8,128)}) %reduce-scatter.7.cloned.1.call-update) | async-done | bytes 131088
  1695.0 3.9 fusion
  1698.9 1.7 fusion.1
  1700.6 2.5 copy.34
  1703.2 83.2 %all-reduce.3.cloned.1.call-done = f32[512,32]{0,1:T(8,128)} async-done(((f32[512,32]{0,1:T(8,128)}), f32[512,32]{0,1:T(8,128)}) %all-reduce.3.cloned.1.call-update) | async-done | bytes 65552 | tf_op jit(solution)/shard_map/psum | solution.py:42
  1786.4 83.4 %reduce-scatter.5.cloned.1.call-done = f32[32,1024]{1,0:T(8,128)} async-done(((f32[32,16384]{1,0:T(8,128)}), f32[32,1024]{1,0:T(8,128)}) %reduce-scatter.5.cloned.1.call-update) | async-done | bytes 131088 | tf_op jit(solution)/shard_map/reduce_scatter | solution.py:54
  1869.8 1.5 copy.46
  (147 shorter events, 21.0 us)
Async XLA Ops:
  8.0 1620.8 %copy-start = (f32[512,32]{0,1:T(8,128)S(1)}, f32[512,32]{0,1:T(8,128)}, u32[]{:S(2)}) copy-start(f32[512,32]{0,1:T(8,128)} %param.9) | copy-start | bytes 196612
  9.5 99.6 %all-reduce.5.cloned.1.call-start = ((), (), s32[]{:S(2)}) async-start(), calls=%async_computation.6 | async-start | bytes 262144 | tf_op jit(solution)/shard_map/while/body/eval_jaxpr/psum | solution.py:11
  110.9 96.4 %all-reduce.5.cloned.1.call-start = ((), (), s32[]{:S(2)}) async-start(), calls=%async_computation.6 | async-start | bytes 262144 | tf_op jit(solution)/shard_map/while/body/eval_jaxpr/psum | solution.py:11
  209.2 96.4 %all-reduce.5.cloned.1.call-start = ((), (), s32[]{:S(2)}) async-start(), calls=%async_computation.6 | async-start | bytes 262144 | tf_op jit(solution)/shard_map/while/body/eval_jaxpr/psum | solution.py:11
  307.4 96.1 %all-reduce.5.cloned.1.call-start = ((), (), s32[]{:S(2)}) async-start(), calls=%async_computation.6 | async-start | bytes 262144 | tf_op jit(solution)/shard_map/while/body/eval_jaxpr/psum | solution.py:11
  405.4 96.1 %all-reduce.5.cloned.1.call-start = ((), (), s32[]{:S(2)}) async-start(), calls=%async_computation.6 | async-start | bytes 262144 | tf_op jit(solution)/shard_map/while/body/eval_jaxpr/psum | solution.py:11
  503.4 96.1 %all-reduce.5.cloned.1.call-start = ((), (), s32[]{:S(2)}) async-start(), calls=%async_computation.6 | async-start | bytes 262144 | tf_op jit(solution)/shard_map/while/body/eval_jaxpr/psum | solution.py:11
  601.3 96.4 %all-reduce.5.cloned.1.call-start = ((), (), s32[]{:S(2)}) async-start(), calls=%async_computation.6 | async-start | bytes 262144 | tf_op jit(solution)/shard_map/while/body/eval_jaxpr/psum | solution.py:11
  699.6 96.4 %all-reduce.5.cloned.1.call-start = ((), (), s32[]{:S(2)}) async-start(), calls=%async_computation.6 | async-start | bytes 262144 | tf_op jit(solution)/shard_map/while/body/eval_jaxpr/psum | solution.py:11
  797.8 96.4 %all-reduce.5.cloned.1.call-start = ((), (), s32[]{:S(2)}) async-start(), calls=%async_computation.6 | async-start | bytes 262144 | tf_op jit(solution)/shard_map/while/body/eval_jaxpr/psum | solution.py:11
  896.1 96.1 %all-reduce.5.cloned.1.call-start = ((), (), s32[]{:S(2)}) async-start(), calls=%async_computation.6 | async-start | bytes 262144 | tf_op jit(solution)/shard_map/while/body/eval_jaxpr/psum | solution.py:11
  994.0 96.4 %all-reduce.5.cloned.1.call-start = ((), (), s32[]{:S(2)}) async-start(), calls=%async_computation.6 | async-start | bytes 262144 | tf_op jit(solution)/shard_map/while/body/eval_jaxpr/psum | solution.py:11
  1092.3 96.1 %all-reduce.5.cloned.1.call-start = ((), (), s32[]{:S(2)}) async-start(), calls=%async_computation.6 | async-start | bytes 262144 | tf_op jit(solution)/shard_map/while/body/eval_jaxpr/psum | solution.py:11
  1190.2 96.4 %all-reduce.5.cloned.1.call-start = ((), (), s32[]{:S(2)}) async-start(), calls=%async_computation.6 | async-start | bytes 262144 | tf_op jit(solution)/shard_map/while/body/eval_jaxpr/psum | solution.py:11
  1288.5 96.1 %all-reduce.5.cloned.1.call-start = ((), (), s32[]{:S(2)}) async-start(), calls=%async_computation.6 | async-start | bytes 262144 | tf_op jit(solution)/shard_map/while/body/eval_jaxpr/psum | solution.py:11
  1386.5 96.1 %all-reduce.5.cloned.1.call-start = ((), (), s32[]{:S(2)}) async-start(), calls=%async_computation.6 | async-start | bytes 262144 | tf_op jit(solution)/shard_map/while/body/eval_jaxpr/psum | solution.py:11
  1484.4 96.1 %all-reduce.5.cloned.1.call-start = ((), (), s32[]{:S(2)}) async-start(), calls=%async_computation.6 | async-start | bytes 262144 | tf_op jit(solution)/shard_map/while/body/eval_jaxpr/psum | solution.py:11
  1582.4 46.4 %all-gather.2.cloned.1.call-start = ((), (), s32[]{:S(2)}) async-start(), calls=%async_computation.2 | async-start | bytes 2228224 | tf_op jit(solution)/shard_map/all_gather | solution.py:37
  1588.5 43.9 %copy-start.2 = (f32[32,1024]{1,0:T(8,128)S(1)}, f32[32,1024]{1,0:T(8,128)}, u32[]{:S(2)}) copy-start(f32[32,1024]{1,0:T(8,128)} %param.10) | copy-start | bytes 393220
  1589.2 104.7 %reduce-scatter.7.cloned.1.call-start = ((), (), s32[]{:S(2)}) async-start(), calls=%async_computation.5 | async-start | bytes 2228224
  1636.1 1.6 copy-start.1
  1636.1 150.3 %all-reduce.3.cloned.1.call-start = ((), (), s32[]{:S(2)}) async-start(), calls=%async_computation.4 | async-start | bytes 131072 | tf_op jit(solution)/shard_map/psum | solution.py:42
  1640.4 229.4 %reduce-scatter.5.cloned.1.call-start = ((), (), s32[]{:S(2)}) async-start(), calls=%async_computation.3 | async-start | bytes 2228224 | tf_op jit(solution)/shard_map/reduce_scatter | solution.py:54
  1695.0 3.9 copy-start.3
Sparse Core Ops, SparseCore 0:
  14.1 94.9 all-reduce.4
  115.6 91.7 all-reduce.4
  213.8 91.7 all-reduce.4
  311.7 91.7 all-reduce.4
  409.7 91.7 all-reduce.4
  507.7 91.7 all-reduce.4
  605.9 91.7 all-reduce.4
  704.2 91.7 all-reduce.4
  802.4 91.7 all-reduce.4
  900.4 91.7 all-reduce.4
  998.6 91.7 all-reduce.4
  1096.6 91.7 all-reduce.4
  1194.9 91.7 all-reduce.4
  1292.8 91.7 all-reduce.4
  1390.8 91.7 all-reduce.4
  1488.7 91.7 all-reduce.4
Sparse Core Ops, SparseCore 1:
  1589.3 39.4 all-gather.1
  1636.2 57.6 reduce-scatter.6
  1697.5 88.9 all-reduce.2
  1791.0 78.8 reduce-scatter.4
where the time goes:
time: 1880 us
  waiting for transfers between devices  1790 us (95%)
  local copies, waits for them, and re-layouts  34.7 us (2%)
  matrix products  19.9 us (1%)
    psum x16, waiting for transfers between devices, from_root(): return lax.psum(kept, axis)  1530 us
    reduce_scatter x1, waiting for transfers between devices, on_device(): lax.psum_scatter(partial_grad, 'node', scatter_dimension=1, tiled=True)  83.4 us
    psum x1, waiting for transfers between devices, on_device(): lax.psum(jnp.dot(mixed_full, grad_pre.T, precision=HIGH), 'node')  83.2 us
    unnamed x5, waiting for transfers between devices  53.5 us
    all_gather x1, waiting for transfers between devices, on_device(): mixed_full = lax.all_gather(mixed_t, 'feat', axis=0, tiled=True)  39.5 us
  transfers between devices with their start and end apart: 20, of which 20 were waited for; matrix products, arithmetic and copies ran while one was open for 1% of the time, Pallas kernels for 0%

commit v1 on v0

--- a/solution.py
+++ b/solution.py
@@ -34,7 +34,10 @@
     mixed_t = jnp.einsum("fbkc,bkrc->fbr", selected, tiles, precision=HIGH).reshape(
         width_part, rows
     )
-    mixed_full = lax.all_gather(mixed_t, "feat", axis=0, tiled=True)
+    size = lax.axis_size("feat")
+    blocks = jnp.stack([mixed_t for _ in range(size)])
+    blocks = lax.all_to_all(blocks, "feat", split_axis=0, concat_axis=0)
+    mixed_full = jnp.concatenate(blocks, axis=0)
     pre_t = jnp.dot(weight.T, mixed_full, precision=HIGH)
     sig = jax.nn.sigmoid(pre_t)
     out_t = pre_t * sig

time: 1880 us -> 1840 us (0.979)
  waiting for transfers between devices: 1790 us -> 1690 us
  blocking collectives: 0 us -> 56.7 us
    psum x1, waiting for transfers between devices: 83.2 us -> 26.2 us  [on_device(): lax.psum(jnp.dot(mixed_full, grad_pre.T, precision=HIGH), 'node')]
    all_to_all x0 -> x1, blocking collectives: none -> 56.7 us  [on_device(): blocks = lax.all_to_all(blocks, 'feat', split_axis=0, concat_axis=0)]
    all_gather x1 -> x0, waiting for transfers between devices: 39.5 us -> none  [on_device(): mixed_full = lax.all_gather(mixed_t, 'feat', axis=0, tiled=True)]
    unnamed x5 -> x4, waiting for transfers between devices: 53.5 us -> 53.6 us
  transfers between devices with their start and end apart: 20 -> 19, of which waited for: 20 -> 19; matrix products, arithmetic and copies ran while one was open for 1% -> 1% of each run, Pallas kernels for 0% -> 0%
where the time goes in v1:
time: 1840 us
  waiting for transfers between devices  1690 us (92%)
  blocking collectives  56.7 us (3%)
  local copies, waits for them, and re-layouts  33.9 us (2%)
  matrix products  19.6 us (1%)
    psum x16, waiting for transfers between devices, from_root(): return lax.psum(kept, axis)  1530 us
    reduce_scatter x1, waiting for transfers between devices, on_device(): lax.psum_scatter(partial_grad, 'node', scatter_dimension=1, tiled=True)  83.2 us
    all_to_all x1, blocking collectives, on_device(): blocks = lax.all_to_all(blocks, 'feat', split_axis=0, concat_axis=0)  56.7 us
    unnamed x4, waiting for transfers between devices  53.6 us
  transfers between devices with their start and end apart: 19, of which 19 were waited for; matrix products, arithmetic and copies ran while one was open for 1% of the time, Pallas kernels for 0%

profile of v1, /device:TPU:2, one launch (start us, length us, event | category | flops | bytes accessed | tf_op | source)
XLA Modules:
  0.0 1837.6 jit_solution(15740148400103368353)
XLA Ops:
  9.5 1572.9 %while.16 = (s32[]{:T(128)}, f32[32,8,8,128]{3,0,2,1:T(8,128)S(1)}, s32[8,8]{1,0:T(8,128)S(1)}, s32[8,8]{1,0:T(8,128)S(1)}, f32[32,1024]{1,0:T(8,128)}, /*index=5*/s32[]{:T(128)}, u32[]{:T(128)}, u32[]{:T(128)}, s32[]{:T(128)}) while((s32[]{:T(128)}, f32[32,8,8,128]{3,0,2,1:T(8,128)S(1)}, s32[8,8]{1,0:T(8,128)S(1)}, ...), condition=%wide.region_2.3_spmd.clone, body=%wide.region_0.2_spmd.clone.sunk | while | flops 853639 | bytes 6298053 | solution.py:32
  10.4 98.7 %all-reduce.5.cloned.1.call-done = f32[32,8,128]{2,0,1:T(8,128)} async-done(((f32[32,8,128]{2,0,1:T(8,128)}), f32[32,8,128]{2,0,1:T(8,128)}) %all-reduce.5.cloned.1.call-update) | async-done | bytes 131088 | tf_op jit(solution)/shard_map/while/body/eval_jaxpr/psum | solution.py:11
  109.1 1.5 gather_fusion
  111.8 95.5 %all-reduce.5.cloned.1.call-done = f32[32,8,128]{2,0,1:T(8,128)} async-done(((f32[32,8,128]{2,0,1:T(8,128)}), f32[32,8,128]{2,0,1:T(8,128)}) %all-reduce.5.cloned.1.call-update) | async-done | bytes 131088 | tf_op jit(solution)/shard_map/while/body/eval_jaxpr/psum | solution.py:11
  207.4 1.5 gather_fusion
  210.1 95.5 %all-reduce.5.cloned.1.call-done = f32[32,8,128]{2,0,1:T(8,128)} async-done(((f32[32,8,128]{2,0,1:T(8,128)}), f32[32,8,128]{2,0,1:T(8,128)}) %all-reduce.5.cloned.1.call-update) | async-done | bytes 131088 | tf_op jit(solution)/shard_map/while/body/eval_jaxpr/psum | solution.py:11
  305.6 1.5 gather_fusion
  308.3 95.2 %all-reduce.5.cloned.1.call-done = f32[32,8,128]{2,0,1:T(8,128)} async-done(((f32[32,8,128]{2,0,1:T(8,128)}), f32[32,8,128]{2,0,1:T(8,128)}) %all-reduce.5.cloned.1.call-update) | async-done | bytes 131088 | tf_op jit(solution)/shard_map/while/body/eval_jaxpr/psum | solution.py:11
  403.6 1.5 gather_fusion
  405.5 1.6 copy_bitcast_fusion.4
  407.2 94.3 %all-reduce.5.cloned.1.call-done = f32[32,8,128]{2,0,1:T(8,128)} async-done(((f32[32,8,128]{2,0,1:T(8,128)}), f32[32,8,128]{2,0,1:T(8,128)}) %all-reduce.5.cloned.1.call-update) | async-done | bytes 131088 | tf_op jit(solution)/shard_map/while/body/eval_jaxpr/psum | solution.py:11
  501.5 1.5 gather_fusion
  504.2 95.2 %all-reduce.5.cloned.1.call-done = f32[32,8,128]{2,0,1:T(8,128)} async-done(((f32[32,8,128]{2,0,1:T(8,128)}), f32[32,8,128]{2,0,1:T(8,128)}) %all-reduce.5.cloned.1.call-update) | async-done | bytes 131088 | tf_op jit(solution)/shard_map/while/body/eval_jaxpr/psum | solution.py:11
  599.5 1.5 gather_fusion
  602.2 95.5 %all-reduce.5.cloned.1.call-done = f32[32,8,128]{2,0,1:T(8,128)} async-done(((f32[32,8,128]{2,0,1:T(8,128)}), f32[32,8,128]{2,0,1:T(8,128)}) %all-reduce.5.cloned.1.call-update) | async-done | bytes 131088 | tf_op jit(solution)/shard_map/while/body/eval_jaxpr/psum | solution.py:11
  697.7 1.5 gather_fusion
  700.5 95.5 %all-reduce.5.cloned.1.call-done = f32[32,8,128]{2,0,1:T(8,128)} async-done(((f32[32,8,128]{2,0,1:T(8,128)}), f32[32,8,128]{2,0,1:T(8,128)}) %all-reduce.5.cloned.1.call-update) | async-done | bytes 131088 | tf_op jit(solution)/shard_map/while/body/eval_jaxpr/psum | solution.py:11
  796.0 1.5 gather_fusion
  798.7 95.5 %all-reduce.5.cloned.1.call-done = f32[32,8,128]{2,0,1:T(8,128)} async-done(((f32[32,8,128]{2,0,1:T(8,128)}), f32[32,8,128]{2,0,1:T(8,128)}) %all-reduce.5.cloned.1.call-update) | async-done | bytes 131088 | tf_op jit(solution)/shard_map/while/body/eval_jaxpr/psum | solution.py:11
  894.2 1.5 gather_fusion
  897.0 95.2 %all-reduce.5.cloned.1.call-done = f32[32,8,128]{2,0,1:T(8,128)} async-done(((f32[32,8,128]{2,0,1:T(8,128)}), f32[32,8,128]{2,0,1:T(8,128)}) %all-reduce.5.cloned.1.call-update) | async-done | bytes 131088 | tf_op jit(solution)/shard_map/while/body/eval_jaxpr/psum | solution.py:11
  992.2 1.5 gather_fusion
  994.9 95.5 %all-reduce.5.cloned.1.call-done = f32[32,8,128]{2,0,1:T(8,128)} async-done(((f32[32,8,128]{2,0,1:T(8,128)}), f32[32,8,128]{2,0,1:T(8,128)}) %all-reduce.5.cloned.1.call-update) | async-done | bytes 131088 | tf_op jit(solution)/shard_map/while/body/eval_jaxpr/psum | solution.py:11
  1090.4 1.5 gather_fusion
  1093.2 95.2 %all-reduce.5.cloned.1.call-done = f32[32,8,128]{2,0,1:T(8,128)} async-done(((f32[32,8,128]{2,0,1:T(8,128)}), f32[32,8,128]{2,0,1:T(8,128)}) %all-reduce.5.cloned.1.call-update) | async-done | bytes 131088 | tf_op jit(solution)/shard_map/while/body/eval_jaxpr/psum | solution.py:11
  1188.4 1.5 gather_fusion
  1191.1 95.5 %all-reduce.5.cloned.1.call-done = f32[32,8,128]{2,0,1:T(8,128)} async-done(((f32[32,8,128]{2,0,1:T(8,128)}), f32[32,8,128]{2,0,1:T(8,128)}) %all-reduce.5.cloned.1.call-update) | async-done | bytes 131088 | tf_op jit(solution)/shard_map/while/body/eval_jaxpr/psum | solution.py:11
  1286.7 1.5 gather_fusion
  1289.4 95.2 %all-reduce.5.cloned.1.call-done = f32[32,8,128]{2,0,1:T(8,128)} async-done(((f32[32,8,128]{2,0,1:T(8,128)}), f32[32,8,128]{2,0,1:T(8,128)}) %all-reduce.5.cloned.1.call-update) | async-done | bytes 131088 | tf_op jit(solution)/shard_map/while/body/eval_jaxpr/psum | solution.py:11
  1384.6 1.5 gather_fusion
  1387.3 95.2 %all-reduce.5.cloned.1.call-done = f32[32,8,128]{2,0,1:T(8,128)} async-done(((f32[32,8,128]{2,0,1:T(8,128)}), f32[32,8,128]{2,0,1:T(8,128)}) %all-reduce.5.cloned.1.call-update) | async-done | bytes 131088 | tf_op jit(solution)/shard_map/while/body/eval_jaxpr/psum | solution.py:11
  1482.6 1.5 gather_fusion
  1485.3 95.2 %all-reduce.5.cloned.1.call-done = f32[32,8,128]{2,0,1:T(8,128)} async-done(((f32[32,8,128]{2,0,1:T(8,128)}), f32[32,8,128]{2,0,1:T(8,128)}) %all-reduce.5.cloned.1.call-update) | async-done | bytes 131088 | tf_op jit(solution)/shard_map/while/body/eval_jaxpr/psum | solution.py:11
  1580.5 1.5 gather_fusion
  1582.4 6.1 convolution_bitcast_fusion.1
  1588.8 56.7 %all_to_all.5 = f32[16,32,1024]{2,1,0:T(8,128)S(1)} all-to-all(f32[16,32,1024]{2,1,0:T(8,128)S(1)} %stack.3), channel_id=1, replica_groups=mesh['node'=16,'feat'=16] {'feat'}, dimensions={0} | all-to-all | bytes 4194304 | tf_op jit(solution)/shard_map/all_to_all | solution.py:39
  1645.4 2.0 fusion.5
  1647.5 3.2 convolution_bitcast_fusion
  1650.6 2.9 copy.24
  1653.7 2.7 fusion.12
  1656.5 53.5 %reduce-scatter.7.cloned.1.call-done = f32[32,1024]{1,0:T(8,128)} async-done(((f32[512,1024]{1,0:T(8,128)}), f32[32,1024]{1,0:T(8,128)}) %reduce-scatter.7.cloned.1.call-update) | async-done | bytes 131088
  1710.0 1.1 copy.25
  1711.1 3.9 fusion
  1715.1 1.7 fusion.1
  1716.8 2.6 copy.34
  1719.3 26.2 %all-reduce.3.cloned.1.call-done = f32[512,32]{0,1:T(8,128)} async-done(((f32[512,32]{0,1:T(8,128)}), f32[512,32]{0,1:T(8,128)}) %all-reduce.3.cloned.1.call-update) | async-done | bytes 65552 | tf_op jit(solution)/shard_map/psum | solution.py:45
  1745.5 83.2 %reduce-scatter.5.cloned.1.call-done = f32[32,1024]{1,0:T(8,128)} async-done(((f32[32,16384]{1,0:T(8,128)}), f32[32,1024]{1,0:T(8,128)}) %reduce-scatter.5.cloned.1.call-update) | async-done | bytes 131088 | tf_op jit(solution)/shard_map/reduce_scatter | solution.py:57
  1828.7 1.5 copy.46
  (144 shorter events, 19.4 us)
Async XLA Ops:
  8.0 1637.4 %copy-start = (f32[512,32]{0,1:T(8,128)S(1)}, f32[512,32]{0,1:T(8,128)}, u32[]{:S(2)}) copy-start(f32[512,32]{0,1:T(8,128)} %param.9) | copy-start | bytes 196612
  9.5 99.6 %all-reduce.5.cloned.1.call-start = ((), (), s32[]{:S(2)}) async-start(), calls=%async_computation.6 | async-start | bytes 262144 | tf_op jit(solution)/shard_map/while/body/eval_jaxpr/psum | solution.py:11
  110.9 96.4 %all-reduce.5.cloned.1.call-start = ((), (), s32[]{:S(2)}) async-start(), calls=%async_computation.6 | async-start | bytes 262144 | tf_op jit(solution)/shard_map/while/body/eval_jaxpr/psum | solution.py:11
  209.2 96.4 %all-reduce.5.cloned.1.call-start = ((), (), s32[]{:S(2)}) async-start(), calls=%async_computation.6 | async-start | bytes 262144 | tf_op jit(solution)/shard_map/while/body/eval_jaxpr/psum | solution.py:11
  307.4 96.1 %all-reduce.5.cloned.1.call-start = ((), (), s32[]{:S(2)}) async-start(), calls=%async_computation.6 | async-start | bytes 262144 | tf_op jit(solution)/shard_map/while/body/eval_jaxpr/psum | solution.py:11
  405.4 96.1 %all-reduce.5.cloned.1.call-start = ((), (), s32[]{:S(2)}) async-start(), calls=%async_computation.6 | async-start | bytes 262144 | tf_op jit(solution)/shard_map/while/body/eval_jaxpr/psum | solution.py:11
  503.4 96.1 %all-reduce.5.cloned.1.call-start = ((), (), s32[]{:S(2)}) async-start(), calls=%async_computation.6 | async-start | bytes 262144 | tf_op jit(solution)/shard_map/while/body/eval_jaxpr/psum | solution.py:11
  601.3 96.4 %all-reduce.5.cloned.1.call-start = ((), (), s32[]{:S(2)}) async-start(), calls=%async_computation.6 | async-start | bytes 262144 | tf_op jit(solution)/shard_map/while/body/eval_jaxpr/psum | solution.py:11
  699.6 96.4 %all-reduce.5.cloned.1.call-start = ((), (), s32[]{:S(2)}) async-start(), calls=%async_computation.6 | async-start | bytes 262144 | tf_op jit(solution)/shard_map/while/body/eval_jaxpr/psum | solution.py:11
  797.8 96.4 %all-reduce.5.cloned.1.call-start = ((), (), s32[]{:S(2)}) async-start(), calls=%async_computation.6 | async-start | bytes 262144 | tf_op jit(solution)/shard_map/while/body/eval_jaxpr/psum | solution.py:11
  896.1 96.1 %all-reduce.5.cloned.1.call-start = ((), (), s32[]{:S(2)}) async-start(), calls=%async_computation.6 | async-start | bytes 262144 | tf_op jit(solution)/shard_map/while/body/eval_jaxpr/psum | solution.py:11
  994.0 96.4 %all-reduce.5.cloned.1.call-start = ((), (), s32[]{:S(2)}) async-start(), calls=%async_computation.6 | async-start | bytes 262144 | tf_op jit(solution)/shard_map/while/body/eval_jaxpr/psum | solution.py:11
  1092.3 96.1 %all-reduce.5.cloned.1.call-start = ((), (), s32[]{:S(2)}) async-start(), calls=%async_computation.6 | async-start | bytes 262144 | tf_op jit(solution)/shard_map/while/body/eval_jaxpr/psum | solution.py:11
  1190.2 96.4 %all-reduce.5.cloned.1.call-start = ((), (), s32[]{:S(2)}) async-start(), calls=%async_computation.6 | async-start | bytes 262144 | tf_op jit(solution)/shard_map/while/body/eval_jaxpr/psum | solution.py:11
  1288.5 96.1 %all-reduce.5.cloned.1.call-start = ((), (), s32[]{:S(2)}) async-start(), calls=%async_computation.6 | async-start | bytes 262144 | tf_op jit(solution)/shard_map/while/body/eval_jaxpr/psum | solution.py:11
  1386.5 96.1 %all-reduce.5.cloned.1.call-start = ((), (), s32[]{:S(2)}) async-start(), calls=%async_computation.6 | async-start | bytes 262144 | tf_op jit(solution)/shard_map/while/body/eval_jaxpr/psum | solution.py:11
  1484.4 96.1 %all-reduce.5.cloned.1.call-start = ((), (), s32[]{:S(2)}) async-start(), calls=%async_computation.6 | async-start | bytes 262144 | tf_op jit(solution)/shard_map/while/body/eval_jaxpr/psum | solution.py:11
  1582.4 127.6 %reduce-scatter.7.cloned.1.call-start = ((), (), s32[]{:S(2)}) async-start(), calls=%async_computation.5 | async-start | bytes 2228224
  1645.4 2.0 copy-start.1
  1653.6 91.9 %all-reduce.3.cloned.1.call-start = ((), (), s32[]{:S(2)}) async-start(), calls=%async_computation.4 | async-start | bytes 131072 | tf_op jit(solution)/shard_map/psum | solution.py:45
  1656.4 172.3 %reduce-scatter.5.cloned.1.call-start = ((), (), s32[]{:S(2)}) async-start(), calls=%async_computation.3 | async-start | bytes 2228224 | tf_op jit(solution)/shard_map/reduce_scatter | solution.py:57
  1711.1 3.9 copy-start.2
Sparse Core Ops, SparseCore 0:
  14.1 94.9 all-reduce.4
  115.6 91.7 all-reduce.4
  213.8 91.7 all-reduce.4
  311.7 91.7 all-reduce.4
  409.7 91.7 all-reduce.4
  507.7 91.7 all-reduce.4
  605.9 91.7 all-reduce.4
  704.2 91.7 all-reduce.4
  802.4 91.7 all-reduce.4
  900.4 91.7 all-reduce.4
  998.6 91.7 all-reduce.4
  1096.6 91.7 all-reduce.4
  1194.9 91.7 all-reduce.4
  1292.8 91.7 all-reduce.4
  1390.8 91.7 all-reduce.4
  1488.7 91.7 all-reduce.4
  1657.9 87.5 all-reduce.2
  1749.9 78.7 reduce-scatter.4
Sparse Core Ops, SparseCore 1:
  1653.7 56.2 reduce-scatter.6
